TPU v7x, 512 devices: a whole 4x8x8 slice. The times are simulated.
512 devices in a mesh: ct: 128 (over y, z, core), bl: 4 (over x).
Axes of the slice: x: 4, y: 8, z: 8, core: 2. Of those that a mesh axis runs over, the one named last changes fastest.
Arguments:
- samples: bfloat16 [1024, 65536], P('ct', 'bl'), may hold values from -6 to 6
- history: bfloat16 [1024, 1536], P('ct'), may hold values from -6 to 6
- tile_cell: int32 [256, 36], P('ct'), may hold values from 0 to 7
- tile_weight: float32 [256, 36], P('ct'), may hold values from 0.25 to 4
Outputs:
- grid: float32 [8, 256, 2, 128, 128], P('bl', 'ct')
All inputs are finite; a program needn't handle non-finite values.
Results may differ from a plain program's by a relative error of at most 0.0048.
Values may be sent and summed in bfloat16 or wider, within the bound.
A program may use at most 64 MiB of HBM per device.

v0:
```python
import math
import jax
import jax.numpy as jnp
from jax import lax
from jax.sharding import PartitionSpec as P

CH = 256
BLOCK = 128
TAPS = 4
SPECTRA = 128
CELL_DEV = 2
FRAME = 512


def from_behind(value, axis, by):
    size = lax.axis_size(axis)
    pairs = [(i, i + by) for i in range(size) if 0 <= i + by < size]
    return lax.ppermute(value, axis, pairs)


def filter_table():
    span = TAPS * FRAME
    sample_pos = jnp.arange(span, dtype=jnp.float32) + 0.5
    window = jnp.sinc(sample_pos / FRAME - TAPS / 2.0) * (
        0.5 - 0.5 * jnp.cos(2.0 * math.pi * sample_pos / span)
    )
    phase_int = (
        jnp.arange(FRAME, dtype=jnp.int32)[:, None]
        * jnp.arange(CH, dtype=jnp.int32)[None, :]
        % FRAME
    )
    angle = phase_int.astype(jnp.float32) * (2.0 * math.pi / FRAME)
    basis = jnp.concatenate([jnp.cos(angle), -jnp.sin(angle)], axis=1)
    table = window.reshape(TAPS, FRAME)[:, :, None] * basis[None] * (2.0 / math.sqrt(FRAME))
    return table.astype(jnp.bfloat16)


def cell_selector(tile_cell, weights, tri_index, is_valid, cell_count):
    picked = jnp.take(tile_cell, tri_index, axis=1)
    picked_weight = jnp.take(weights, tri_index, axis=1) * is_valid
    cell_ids = lax.broadcasted_iota(jnp.int32, (cell_count, 1, 1), 0)
    return (picked[None] == cell_ids).astype(jnp.float32) * picked_weight[None]


def shards(samples, history, tile_cell, tile_weight):
    bl_size = lax.axis_size("bl")
    bl_index = lax.axis_index("bl")
    inputs_dev = samples.shape[0]
    spec_dev = samples.shape[1] // FRAME
    table = filter_table()
    frames = samples.reshape(inputs_dev, spec_dev, FRAME)
    last_frames = frames[:, spec_dev - (TAPS - 1) :, :]
    earlier = from_behind(last_frames, "bl", 1)
    earlier = jnp.where(bl_index == 0, history.reshape(inputs_dev, TAPS - 1, FRAME), earlier)
    extended = jnp.concatenate([earlier, frames], axis=1)
    accum = jnp.zeros((2 * CH, inputs_dev, spec_dev), jnp.float32)
    for tap_index in range(TAPS):
        accum = accum + jnp.einsum(
            "psn,nk->kps",
            extended[:, tap_index : tap_index + spec_dev],
            table[tap_index],
            preferred_element_type=jnp.float32,
        )
    spectra = accum.astype(jnp.bfloat16).reshape(2, CH, inputs_dev, spec_dev)
    turned = lax.all_to_all(spectra, "ct", split_axis=1, concat_axis=2, tiled=True)
    channels = turned.shape[1]
    inputs = turned.shape[2]
    blocks = inputs // BLOCK
    cell_count = CELL_DEV * bl_size
    weights = tile_weight * (1.0 / math.sqrt(SPECTRA))
    rows_each = blocks // bl_size
    shard_part = lax.all_gather(turned, "bl", axis=3, tiled=True)
    row_part = lax.dynamic_slice_in_dim(
        shard_part, bl_index * rows_each * BLOCK, rows_each * BLOCK, 2
    )
    products = jnp.einsum(
        "acps,bcqs->cabpq", row_part, shard_part, preferred_element_type=jnp.float32
    )
    visibility = jnp.stack(
        [products[:, 0, 0] + products[:, 1, 1], products[:, 1, 0] - products[:, 0, 1]], axis=1
    )
    visibility = visibility.reshape(channels, 2, rows_each, BLOCK, blocks, BLOCK)
    row_index = bl_index * rows_each + jnp.arange(rows_each, dtype=jnp.int32)
    col_index = jnp.arange(blocks, dtype=jnp.int32)
    is_valid = col_index[None, :] >= row_index[:, None]
    tri_index = (
        row_index[:, None] * blocks
        - row_index[:, None] * (row_index[:, None] - 1) // 2
        + col_index[None, :]
        - row_index[:, None]
    )
    tri_index = jnp.where(is_valid, tri_index, 0).reshape(-1)
    selector = cell_selector(
        tile_cell, weights, tri_index, is_valid.reshape(-1).astype(jnp.float32), cell_count
    )
    selector = selector.reshape(cell_count, channels, rows_each, blocks)
    cell_term = jnp.einsum(
        "ecmj,cxmpjq->ecxpq", selector, visibility, precision=lax.Precision.HIGHEST
    )
    return lax.psum_scatter(cell_term, "bl", scatter_dimension=0, tiled=True)


def solution(mesh):
    return jax.shard_map(
        shards,
        mesh=mesh,
        in_specs=(P("ct", "bl"), P("ct", None), P("ct", None), P("ct", None)),
        out_specs=P("bl", "ct", None, None, None),
        check_vma=False,
    )
```

profile of v0, /device:TPU:1, one launch (start us, length us, event | category | flops | bytes accessed | tf_op | source)
XLA Modules:
  0.0 138.1 jit_solution(12725136759354073979)
XLA Ops:
  6.5 1.0 copy.82
  7.6 3.9 %collective-permute-start = (bf16[8,3,512]{2,1,0:T(4,128)(2,1)S(1)}, bf16[8,3,512]{2,1,0:T(4,128)(2,1)S(1)}, u32[]{:S(2)}, u32[]{:S(2)}) collective-permute-start(bf16[8,3,512]{2,1,0:T(4,128)(2,1)S(1)} %slice.53), channel_id=1, source_target_pairs={{0,1},{1,2},{2,3},{4,5},{5,6},{6,7},{8,9},{9,10},{10,11},{12,13},{... | collective-permute-start | bytes 73736 | tf_op jit(solution)/shard_map/ppermute | solution.py:18
  11.6 2.1 %sine_negate_fusion = (f32[512,256]{1,0:T(8,128)S(1)}, f32[512,256]{1,0:T(8,128)S(1)}) fusion(), kind=kLoop, calls=%fused_computation.30 | loop fusion | flops 1966080 | bytes 1048576 | tf_op jit(solution)/shard_map/neg | solution.py:33
  13.9 0.4 multiply_convert_fusion
  14.3 0.5 copy-done
  15.2 0.4 copy-done.1
  16.7 1.1 copy.52
  17.8 0.8 reshape.324
  18.6 32.0 %all_to_all.18 = bf16[128,2,512]{2,1,0:T(2,128)(2,1)S(1)} all-to-all(bf16[128,2,512]{2,1,0:T(2,128)(2,1)S(1)} %reshape.324), channel_id=1, replica_groups=mesh['ct'=128,'bl'=4] {'ct'}, dimensions={0} | all-to-all | bytes 524288 | tf_op jit(solution)/shard_map/all_to_all | solution.py:65
  50.6 0.5 reshape.325
  51.3 1.2 copy.55
  53.3 0.6 gather_fusion.1
  54.0 0.6 gather_fusion
  54.8 19.1 %all-gather.2.cloned.1.call-done = bf16[2,2,1024,128]{2,1,0,3:T(2,128)(2,1)} async-done(((bf16[2,2,1024,32]{2,1,0,3:T(2,128)(2,1)}), bf16[2,2,1024,128]{2,1,0,3:T(2,128)(2,1)}) %all-gather.2.cloned.1.call-update) | async-done | bytes 1048592 | tf_op jit(solution)/shard_map/all_gather | solution.py:72
  73.9 1.1 constant_dynamic-slice_fusion
  75.3 2.5 %convolution_bitcast_fusion = f32[2,2,2,256,1024]{3,4,1,2,0:T(8,128)S(1)} fusion(bf16[2,2,1024,128,1]{2,1,0,3,4:T(2,128)(2,1)} %bitcast.68, bf16[2,2,256,128]{3,2,0,1:T(8,128)(2,1)S(1)} %copy.74), kind=kOutput, calls=%fused_computation.7 | convolution fusion | flops 536870912 | bytes 9699328 | tf_op jit(solution)/shard_map/acps,bcqs->cabpq/dot_general | solution.py:76
  77.8 2.5 %slice_add_fusion = (f32[2,1,1,256,1024]{3,4,1,2,0:T(8,128)}, f32[2,1,1,256,1024]{3,4,1,2,0:T(8,128)}) fusion(f32[2,2,2,256,1024]{3,4,1,2,0:T(8,128)S(1)} %convolution_bitcast_fusion), kind=kLoop, calls=%fused_computation.9 | loop fusion | flops 1048576 | bytes 12582912 | tf_op jit(solution)/shard_map/add | solution.py:80
  80.3 2.3 %add.221 = f32[2,1,2,128,8,128]{3,2,5,4,0,1:T(2,128)S(1)} reshape(f32[2,1,1,256,1024]{3,4,1,2,0:T(8,128)} %get-tuple-element.5) | data formatting | bytes 4194304 | tf_op jit(solution)/shard_map/add | solution.py:80
  82.6 2.0 %copy.58 = f32[2,1,2,128,8,128]{5,4,2,3,1,0:T(8,128)} copy(f32[2,1,2,128,8,128]{3,2,5,4,0,1:T(2,128)S(1)} %add.221) | data formatting | bytes 4194304 | tf_op jit(solution)/shard_map/add | solution.py:80
  84.6 2.3 %sub.83 = f32[2,1,2,128,8,128]{3,2,5,4,0,1:T(2,128)S(1)} reshape(f32[2,1,1,256,1024]{3,4,1,2,0:T(8,128)} %get-tuple-element.6) | data formatting | bytes 4194304 | tf_op jit(solution)/shard_map/sub | solution.py:80
  86.9 2.0 %copy.59 = f32[2,1,2,128,8,128]{5,4,2,3,1,0:T(8,128)} copy(f32[2,1,2,128,8,128]{3,2,5,4,0,1:T(2,128)S(1)} %sub.83) | data formatting | bytes 4194304 | tf_op jit(solution)/shard_map/sub | solution.py:80
  89.0 4.0 %fusion.4 = f32[8,2,2,128,128]{4,0,3,2,1:T(8,128)S(1)} fusion(f32[2,1,2,128,8,128]{5,4,2,3,1,0:T(8,128)} %copy.59, f32[2,1,2,128,8,128]{5,4,2,3,1,0:T(8,128)} %copy.58, f32[2,2,8]{2,1,0:T(2,128)S(1)} %select_multiply_fusion, s32[2,2,8]{2,1,0:T(2,128)S(1)} %broadcast_select_fusion.1), kind=kOutput, calls=%fused_computation.10 | convolution fusion | flops 101712384 | bytes 6291712 | tf_op jit(solution)/shard_map/ecmj,cxmpjq->ecxpq/dot_general | solution.py:97
  93.0 1.7 %copy.64 = f32[8,2,2,128,128]{4,3,2,1,0:T(8,128)} copy(f32[8,2,2,128,128]{4,0,3,2,1:T(8,128)S(1)} %fusion.4) | data formatting | bytes 4194304 | tf_op jit(solution)/shard_map/ecmj,cxmpjq->ecxpq/transpose | solution.py:97
  94.7 36.5 %reduce-scatter.2.cloned.1.call-done = f32[2,2,2,128,128]{4,3,2,1,0:T(8,128)} async-done(((f32[8,2,2,128,128]{4,3,2,1,0:T(8,128)}), f32[2,2,2,128,128]{4,3,2,1,0:T(8,128)}) %reduce-scatter.2.cloned.1.call-update) | async-done | bytes 524304 | tf_op jit(solution)/shard_map/reduce_scatter | solution.py:100
  (40 shorter events, 3.2 us)
Async XLA Ops:
  6.5 67.4 %all-gather.2.cloned.1.call-start = ((), (), s32[]{:S(2)}) async-start(), calls=%async_computation.2 | async-start | bytes 1310720 | tf_op jit(solution)/shard_map/all_gather | solution.py:72
  7.6 8.0 %collective-permute-start = (bf16[8,3,512]{2,1,0:T(4,128)(2,1)S(1)}, bf16[8,3,512]{2,1,0:T(4,128)(2,1)S(1)}, u32[]{:S(2)}, u32[]{:S(2)}) collective-permute-start(bf16[8,3,512]{2,1,0:T(4,128)(2,1)S(1)} %slice.53), channel_id=1, source_target_pairs={{0,1},{1,2},{2,3},{4,5},{5,6},{6,7},{8,9},{9,10},{10,11},{12,13},{... | collective-permute-start | bytes 73736 | tf_op jit(solution)/shard_map/ppermute | solution.py:18
  13.9 1.0 copy-start
  14.8 0.7 copy-start.1
  51.1 2.1 %copy-start.2 = (f32[2,36]{1,0:T(2,128)S(1)}, f32[2,36]{1,0:T(2,128)}, u32[]{:S(2)}) copy-start(f32[2,36]{1,0:T(2,128)} %param.7) | copy-start | bytes 868
  51.1 2.8 %copy-start.3 = (s32[2,36]{1,0:T(2,128)S(1)}, s32[2,36]{1,0:T(2,128)}, u32[]{:S(2)}) copy-start(s32[2,36]{1,0:T(2,128)} %param.6) | copy-start | bytes 868
  52.5 78.7 %reduce-scatter.2.cloned.1.call-start = ((), (), s32[]{:S(2)}) async-start(), calls=%async_computation.3 | async-start | bytes 2621440 | tf_op jit(solution)/shard_map/reduce_scatter | solution.py:100
Sparse Core Ops, SparseCore 0:
  52.6 21.2 all-gather.1
  94.9 36.3 reduce-scatter.1
where the time goes:
time: 138 us
  waiting for transfers between devices  55.6 us (40%)
  blocking collectives  32 us (23%)
  local copies, waits for them, and re-layouts  19.5 us (14%)
  between operations  13.6 us (10%)
  matrix products  7.79 us (6%)
  other arithmetic  5.36 us (4%)
  starting transfers between devices  4.17 us (3%)
    reduce_scatter x1, waiting for transfers between devices, shards(): return lax.psum_scatter(cell_term, 'bl', scatter_dimension=0, tiled=True)  36.5 us
    all_to_all x1, blocking collectives, shards(): lax.all_to_all(spectra, 'ct', split_axis=1, concat_axis=2, tiled=True)  32 us
    all_gather x1, waiting for transfers between devices, shards(): shard_part = lax.all_gather(turned, 'bl', axis=3, tiled=True)  19.1 us
    sub x2, local copies, waits for them, and re-layouts, shards(): products[:, 1, 0] - products[:, 0, 1]  4.33 us
    add x2, local copies, waits for them, and re-layouts, shards(): products[:, 0, 0] + products[:, 1, 1]  4.33 us
    dot_general x1, matrix products, shards(): jnp.einsum('ecmj,cxmpjq->ecxpq', selector, visibility, precision=lax.Prec...  4.02 us
    ppermute x1, starting transfers between devices, from_behind(): return lax.ppermute(value, axis, pairs)  3.95 us
    unnamed x13, local copies, waits for them, and re-layouts  3.65 us
  transfers between devices with their start and end apart: 3, of which 2 were waited for; matrix products, arithmetic and copies ran while one was open for 4% of the time, Pallas kernels for 0%

commit v1 on v0

--- a/solution.py
+++ b/solution.py
@@ -69,7 +69,10 @@
     cell_count = CELL_DEV * bl_size
     weights = tile_weight * (1.0 / math.sqrt(SPECTRA))
     rows_each = blocks // bl_size
-    shard_part = lax.all_gather(turned, "bl", axis=3, tiled=True)
+    w1 = jnp.stack([turned] * lax.axis_size("bl"))
+    shard_part = jnp.concatenate(
+        lax.all_to_all(w1, axis_name="bl", split_axis=0, concat_axis=0), axis=3
+    )
     row_part = lax.dynamic_slice_in_dim(
         shard_part, bl_index * rows_each * BLOCK, rows_each * BLOCK, 2
     )

time: 138 us -> 125 us (0.906)
  blocking collectives: 32 us -> 0 us
  starting transfers between devices: 4.17 us -> 25.6 us
  waiting for transfers between devices: 55.6 us -> 54.2 us
    all_to_all x1 -> x0, blocking collectives: 32 us -> none  [shards(): lax.all_to_all(spectra, 'ct', split_axis=1, concat_axis=2, tiled=True)]
    all_to_all x0 -> x2, waiting for transfers between devices: none -> 25.2 us  [the longest x1 13.8 us: shards(): lax.all_to_all(spectra, 'ct', split_axis=1, concat_axis=2, tiled=True)]
    all_to_all x0 -> x2, starting transfers between devices: none -> 21.6 us  [the longest x1 17.9 us: shards(): lax.all_to_all(spectra, 'ct', split_axis=1, concat_axis=2, tiled=True)]
    all_gather x1 -> x0, waiting for transfers between devices: 19.1 us -> none  [shards(): shard_part = lax.all_gather(turned, 'bl', axis=3, tiled=True)]
    reduce_scatter x1, waiting for transfers between devices: 36.5 us -> 29 us  [shards(): return lax.psum_scatter(cell_term, 'bl', scatter_dimension=0, tiled=True)]
    another operation x0 -> x2, local copies, waits for them, and re-layouts: none -> 1.43 us  [shards(): w1 = jnp.stack([turned] * lax.axis_size('bl'))]
  transfers between devices with their start and end apart: 3 -> 4, of which waited for: 2 -> 3; matrix products, arithmetic and copies ran while one was open for 4% -> 4% of each run, Pallas kernels for 0% -> 0%
where the time goes in v1:
time: 125 us
  waiting for transfers between devices  54.2 us (43%)
  starting transfers between devices  25.6 us (20%)
  local copies, waits for them, and re-layouts  19.4 us (16%)
  between operations  13.6 us (11%)
  matrix products  6.56 us (5%)
  other arithmetic  5.35 us (4%)
    reduce_scatter x1, waiting for transfers between devices, shards(): return lax.psum_scatter(cell_term, 'bl', scatter_dimension=0, tiled=True)  29 us
    all_to_all x1, starting transfers between devices, shards(): lax.all_to_all(spectra, 'ct', split_axis=1, concat_axis=2, tiled=True)  17.9 us
    all_to_all x1, waiting for transfers between devices, shards(): lax.all_to_all(spectra, 'ct', split_axis=1, concat_axis=2, tiled=True)  13.8 us
    all_to_all x1, waiting for transfers between devices, shards(): lax.all_to_all(w1, axis_name='bl', split_axis=0, concat_axis=0)  11.4 us
    sub x2, local copies, waits for them, and re-layouts, shards(): products[:, 1, 0] - products[:, 0, 1]  4.33 us
    add x2, local copies, waits for them, and re-layouts, shards(): products[:, 0, 0] + products[:, 1, 1]  4.33 us
    unnamed x13, local copies, waits for them, and re-layouts  4.3 us
    dot_general x1, matrix products, shards(): jnp.einsum('ecmj,cxmpjq->ecxpq', selector, visibility, precision=lax.Prec...  4.02 us
  transfers between devices with their start and end apart: 4, of which 3 were waited for; matrix products, arithmetic and copies ran while one was open for 4% of the time, Pallas kernels for 0%

profile of v1, /device:TPU:1, one launch (start us, length us, event | category | flops | bytes accessed | tf_op | source)
XLA Modules:
  0.0 124.8 jit_solution(3029321702172215120)
XLA Ops:
  6.5 1.0 copy.72
  7.6 3.9 %collective-permute-start = (bf16[8,3,512]{2,1,0:T(4,128)(2,1)S(1)}, bf16[8,3,512]{2,1,0:T(4,128)(2,1)S(1)}, u32[]{:S(2)}, u32[]{:S(2)}) collective-permute-start(bf16[8,3,512]{2,1,0:T(4,128)(2,1)S(1)} %slice.53), channel_id=1, source_target_pairs={{0,1},{1,2},{2,3},{4,5},{5,6},{6,7},{8,9},{9,10},{10,11},{12,13},{... | collective-permute-start | bytes 73736 | tf_op jit(solution)/shard_map/ppermute | solution.py:18
  11.6 2.1 %sine_negate_fusion = (f32[512,256]{1,0:T(8,128)S(1)}, f32[512,256]{1,0:T(8,128)S(1)}) fusion(), kind=kLoop, calls=%fused_computation.30 | loop fusion | flops 1966080 | bytes 1048576 | tf_op jit(solution)/shard_map/neg | solution.py:33
  14.3 0.5 copy-done
  15.2 0.4 copy-done.1
  16.7 1.1 copy.41
  17.8 1.5 %reshape.335 = bf16[128,2,512]{2,1,0:T(2,128)(2,1)} reshape(bf16[256,2,8,32]{3,2,1,0:T(8,128)(2,1)S(1)} %bitcast.71) | data formatting | bytes 524288
  19.3 17.9 %all-to-all-start = ((bf16[128,2,512]{2,1,0:T(2,128)(2,1)}), bf16[128,2,512]{2,1,0:T(2,128)(2,1)S(1)}, u32[]{:S(2)}, u32[]{:S(2)}) async-start(bf16[128,2,512]{2,1,0:T(2,128)(2,1)} %reshape.335), calls=%async_computation | async-start | bytes 524288 | tf_op jit(solution)/shard_map/all_to_all | solution.py:65
  37.6 13.8 %all-to-all-done = bf16[128,2,512]{2,1,0:T(2,128)(2,1)S(1)} async-done(((bf16[128,2,512]{2,1,0:T(2,128)(2,1)}), bf16[128,2,512]{2,1,0:T(2,128)(2,1)S(1)}, u32[]{:S(2)}, u32[]{:S(2)}) %all-to-all-start) | async-done | bytes 262176 | tf_op jit(solution)/shard_map/all_to_all | solution.py:65
  51.4 0.5 reshape.336
  52.5 1.1 stack.7
  53.6 3.7 %all-to-all-start.1 = ((bf16[4,2,2,1024,32]{3,4,2,1,0:T(8,128)(2,1)}), bf16[4,2,2,1024,32]{3,4,2,1,0:T(8,128)(2,1)S(1)}, u32[]{:S(2)}, u32[]{:S(2)}) async-start(bf16[4,2,2,1024,32]{3,4,2,1,0:T(8,128)(2,1)} %stack.7), calls=%async_computation.1 | async-start | bytes 2097152 | tf_op jit(solution)/shard_map/all_to_all | solution.py:74
  57.5 0.6 gather_fusion.1
  58.2 0.6 gather_fusion
  59.0 11.4 %all-to-all-done.1 = bf16[4,2,2,1024,32]{3,4,2,1,0:T(8,128)(2,1)S(1)} async-done(((bf16[4,2,2,1024,32]{3,4,2,1,0:T(8,128)(2,1)}), bf16[4,2,2,1024,32]{3,4,2,1,0:T(8,128)(2,1)S(1)}, u32[]{:S(2)}, u32[]{:S(2)}) %all-to-all-start.1) | async-done | bytes 1048608 | tf_op jit(solution)/shard_map/all_to_all | solution.py:74
  70.7 1.3 %convolution_bitcast_fusion = f32[2,2,2,256,1024]{3,4,1,2,0:T(8,128)S(1)} fusion(bf16[2,2,1024,128,1]{2,3,1,0,4:T(8,128)(2,1)S(1)} %bitcast.70, bf16[2,2,256,128]{3,2,0,1:T(8,128)(2,1)S(1)} %copy.64), kind=kOutput, calls=%fused_computation.7 | convolution fusion | flops 536870912 | bytes 9699328 | tf_op jit(solution)/shard_map/acps,bcqs->cabpq/dot_general | solution.py:79
  72.0 2.5 %slice_add_fusion = (f32[2,1,1,256,1024]{3,4,1,2,0:T(8,128)}, f32[2,1,1,256,1024]{3,4,1,2,0:T(8,128)}) fusion(f32[2,2,2,256,1024]{3,4,1,2,0:T(8,128)S(1)} %convolution_bitcast_fusion), kind=kLoop, calls=%fused_computation.9 | loop fusion | flops 1048576 | bytes 12582912 | tf_op jit(solution)/shard_map/add | solution.py:83
  74.5 2.3 %add.221 = f32[2,1,2,128,8,128]{3,2,5,4,0,1:T(2,128)S(1)} reshape(f32[2,1,1,256,1024]{3,4,1,2,0:T(8,128)} %get-tuple-element.5) | data formatting | bytes 4194304 | tf_op jit(solution)/shard_map/add | solution.py:83
  76.8 2.0 %copy.48 = f32[2,1,2,128,8,128]{5,4,2,3,1,0:T(8,128)} copy(f32[2,1,2,128,8,128]{3,2,5,4,0,1:T(2,128)S(1)} %add.221) | data formatting | bytes 4194304 | tf_op jit(solution)/shard_map/add | solution.py:83
  78.8 2.3 %sub.83 = f32[2,1,2,128,8,128]{3,2,5,4,0,1:T(2,128)S(1)} reshape(f32[2,1,1,256,1024]{3,4,1,2,0:T(8,128)} %get-tuple-element.6) | data formatting | bytes 4194304 | tf_op jit(solution)/shard_map/sub | solution.py:83
  81.1 2.0 %copy.49 = f32[2,1,2,128,8,128]{5,4,2,3,1,0:T(8,128)} copy(f32[2,1,2,128,8,128]{3,2,5,4,0,1:T(2,128)S(1)} %sub.83) | data formatting | bytes 4194304 | tf_op jit(solution)/shard_map/sub | solution.py:83
  83.2 4.0 %fusion.4 = f32[8,2,2,128,128]{4,0,3,2,1:T(8,128)S(1)} fusion(f32[2,1,2,128,8,128]{5,4,2,3,1,0:T(8,128)} %copy.49, f32[2,1,2,128,8,128]{5,4,2,3,1,0:T(8,128)} %copy.48, f32[2,2,8]{2,1,0:T(2,128)S(1)} %select_multiply_fusion, s32[2,2,8]{2,1,0:T(2,128)S(1)} %broadcast_select_fusion.1), kind=kOutput, calls=%fused_computation.10 | convolution fusion | flops 101712384 | bytes 6291712 | tf_op jit(solution)/shard_map/ecmj,cxmpjq->ecxpq/dot_general | solution.py:100
  87.2 1.7 %copy.54 = f32[8,2,2,128,128]{4,3,2,1,0:T(8,128)} copy(f32[8,2,2,128,128]{4,0,3,2,1:T(8,128)S(1)} %fusion.4) | data formatting | bytes 4194304 | tf_op jit(solution)/shard_map/ecmj,cxmpjq->ecxpq/transpose | solution.py:100
  88.9 29.0 %reduce-scatter.2.cloned.1.call-done = f32[2,2,2,128,128]{4,3,2,1,0:T(8,128)} async-done(((f32[8,2,2,128,128]{4,3,2,1,0:T(8,128)}), f32[2,2,2,128,128]{4,3,2,1,0:T(8,128)}) %reduce-scatter.2.cloned.1.call-update) | async-done | bytes 524304 | tf_op jit(solution)/shard_map/reduce_scatter | solution.py:103
  (42 shorter events, 3.8 us)
Async XLA Ops:
  7.6 8.0 %collective-permute-start = (bf16[8,3,512]{2,1,0:T(4,128)(2,1)S(1)}, bf16[8,3,512]{2,1,0:T(4,128)(2,1)S(1)}, u32[]{:S(2)}, u32[]{:S(2)}) collective-permute-start(bf16[8,3,512]{2,1,0:T(4,128)(2,1)S(1)} %slice.53), channel_id=1, source_target_pairs={{0,1},{1,2},{2,3},{4,5},{5,6},{6,7},{8,9},{9,10},{10,11},{12,13},{... | collective-permute-start | bytes 73736 | tf_op jit(solution)/shard_map/ppermute | solution.py:18
  13.9 1.0 copy-start
  14.8 0.7 copy-start.1
  16.6 21.0 %copy-start.2 = (f32[2,36]{1,0:T(2,128)S(1)}, f32[2,36]{1,0:T(2,128)}, u32[]{:S(2)}) copy-start(f32[2,36]{1,0:T(2,128)} %param.7) | copy-start | bytes 868
  19.3 32.1 %all-to-all-start = ((bf16[128,2,512]{2,1,0:T(2,128)(2,1)}), bf16[128,2,512]{2,1,0:T(2,128)(2,1)S(1)}, u32[]{:S(2)}, u32[]{:S(2)}) async-start(bf16[128,2,512]{2,1,0:T(2,128)(2,1)} %reshape.335), calls=%async_computation | async-start | bytes 524288 | tf_op jit(solution)/shard_map/all_to_all | solution.py:65
  52.1 6.0 %copy-start.3 = (s32[2,36]{1,0:T(2,128)S(1)}, s32[2,36]{1,0:T(2,128)}, u32[]{:S(2)}) copy-start(s32[2,36]{1,0:T(2,128)} %param.6) | copy-start | bytes 868
  53.6 16.8 %all-to-all-start.1 = ((bf16[4,2,2,1024,32]{3,4,2,1,0:T(8,128)(2,1)}), bf16[4,2,2,1024,32]{3,4,2,1,0:T(8,128)(2,1)S(1)}, u32[]{:S(2)}, u32[]{:S(2)}) async-start(bf16[4,2,2,1024,32]{3,4,2,1,0:T(8,128)(2,1)} %stack.7), calls=%async_computation.1 | async-start | bytes 2097152 | tf_op jit(solution)/shard_map/all_to_all | solution.py:74
  57.3 60.6 %reduce-scatter.2.cloned.1.call-start = ((), (), s32[]{:S(2)}) async-start(), calls=%async_computation.3 | async-start | bytes 2621440 | tf_op jit(solution)/shard_map/reduce_scatter | solution.py:103
Sparse Core Ops, SparseCore 0:
  89.0 28.8 reduce-scatter.1
